TPU v7x, 32 devices: a whole 2x2x4 slice. The times are simulated.
32 devices in a mesh: seq: 8 (over z, y), tp: 4 (over x, core).
Axes of the slice: x: 2, y: 2, z: 4, core: 2. Of those that a mesh axis runs over, the one named last changes fastest.
Arguments:
- subsampled: bfloat16 [2048, 4096], P('seq'), may hold values from -6 to 6
- proj_weight: bfloat16 [4096, 1024], P(None, 'tp'), may hold values from -0.09375 to 0.09375
- value_weight: bfloat16 [1024, 1024], P(None, 'tp'), may hold values from -0.1875 to 0.1875
- gate_weight: bfloat16 [1024, 1024], P(None, 'tp'), may hold values from -0.1875 to 0.1875
- conv_kernel: float32 [9, 1024], P(None, 'tp'), may hold values from -2 to 2
- bn_gain: float32 [1024], P('tp'), may hold values from 0.5 to 1.5
- bn_shift: float32 [1024], P('tp'), may hold values from -2 to 2
- down_weight: bfloat16 [1024, 1024], P(None, 'tp'), may hold values from -0.1875 to 0.1875
- clip_frames: int32 [8, 8], replicated, may hold values from 1 to 64, 256 in all within a row
- clip_dest: int32 [8, 8], replicated, may hold values from 0 to 7, each once within a row
- out_grad: bfloat16 [4096, 1024], P('seq', 'tp'), may hold values from -0.13183594 to 0.13183594
Outputs:
- block_out: bfloat16 [4096, 1024], P('seq', 'tp')
- proj_grad: float32 [4096, 1024], P('seq', 'tp')
- value_grad: float32 [1024, 1024], P('seq', 'tp')
- gate_grad: float32 [1024, 1024], P('seq', 'tp')
- down_grad: float32 [1024, 1024], P('seq', 'tp')
- bn_gain_grad: float32 [1024], P('tp')
- bn_shift_grad: float32 [1024], P('tp')
Inputs may be any that keep to these rules, and one draw needn't show every extreme that they name: `clip_frames`: row s holds the frame counts of the 8 clips of owner s, summing to 256; the largest of each row is 64. `clip_dest`: each row is a permutation: owner s sends exactly one clip to every packed shard.
All inputs are finite; a program needn't handle non-finite values.
Results may differ from a plain program's by a relative error of at most 0.0077.
Values may be sent and summed in bfloat16 or wider, within the bound.
A program may use at most 192 MiB of HBM per device.

v0:
```python
import jax
import jax.numpy as jnp
from jax import lax
from jax.sharding import PartitionSpec as P

MOST = 64


def depthwise(field, kernel):
    half = kernel.shape[0] // 2
    length = field.shape[1]
    padded = jnp.pad(field, ((0, 0), (half, half), (0, 0)))
    total = jnp.zeros(field.shape, jnp.float32)
    for offset in range(kernel.shape[0]):
        total = total + kernel[offset] * padded[:, offset : offset + length]
    return total


def depthwise_back(grad, kernel):
    half = kernel.shape[0] // 2
    length = grad.shape[1]
    padded = jnp.pad(grad, ((0, 0), (half, half), (0, 0)))
    total = jnp.zeros(grad.shape, jnp.float32)
    for offset in range(kernel.shape[0]):
        begin = 2 * half - offset
        total = total + kernel[offset] * padded[:, begin : begin + length]
    return total


def contract_rows(left, right):
    return lax.dot_general(
        left, right, (((0,), (0,)), ((), ())), preferred_element_type=jnp.float32
    )


def contract_cols(left, right):
    return lax.dot_general(
        left, right, (((1,), (1,)), ((), ())), preferred_element_type=jnp.float32
    )


def body(
    subsampled,
    proj_weight,
    value_weight,
    gate_weight,
    conv_kernel,
    bn_gain,
    bn_shift,
    down_weight,
    clip_frames,
    clip_dest,
    out_grad,
):
    shards = lax.axis_size("seq")
    seq_index = lax.axis_index("seq")
    tp_index = lax.axis_index("tp")
    own_rows = subsampled.shape[0]
    part_width = proj_weight.shape[1]
    count = float(own_rows * shards)
    clip_lens = lax.dynamic_slice_in_dim(clip_frames, seq_index, 1, 0)[0]
    clip_targets = lax.dynamic_slice_in_dim(clip_dest, seq_index, 1, 0)[0]
    offsets = jnp.cumsum(clip_lens) - clip_lens
    shard_ids = jnp.arange(shards, dtype=jnp.int32)
    match = clip_targets[None, :] == shard_ids[:, None]
    starts = jnp.sum(jnp.where(match, offsets[None, :], 0), axis=1)
    lengths = jnp.sum(jnp.where(match, clip_lens[None, :], 0), axis=1)
    frame_pos = jnp.arange(MOST, dtype=jnp.int32)
    source_rows = jnp.minimum(starts[:, None] + frame_pos[None, :], own_rows - 1).reshape(-1)
    send_valid = (frame_pos[None, :] < lengths[:, None]).reshape(-1, 1)
    projected = jnp.dot(subsampled, proj_weight, preferred_element_type=jnp.float32).astype(
        jnp.bfloat16
    )
    outgoing = jnp.where(
        send_valid, jnp.take(projected, source_rows, axis=0), jnp.zeros((), jnp.bfloat16)
    )
    arrived = lax.all_to_all(
        outgoing.reshape(shards, MOST, part_width), "seq", split_axis=0, concat_axis=0, tiled=True
    )
    hidden_part = arrived.reshape(shards * MOST, part_width)
    hidden_full = lax.all_gather(hidden_part, "tp", axis=1, tiled=True)
    incoming = clip_dest == seq_index
    in_lengths = jnp.sum(jnp.where(incoming, clip_frames, 0), axis=1)
    valid = (frame_pos[None, :] < in_lengths[:, None]).reshape(-1, 1)
    mask = valid.astype(jnp.float32)
    hidden32 = hidden_full.astype(jnp.float32)
    centred = hidden32 - jnp.mean(hidden32, axis=1, keepdims=True)
    sigma = jnp.sqrt(jnp.mean(centred * centred, axis=1, keepdims=True) + 1e-05)
    normed = centred / sigma
    normed16 = normed.astype(jnp.bfloat16)
    value_pre = jnp.dot(normed16, value_weight, preferred_element_type=jnp.float32)
    gate_pre = jnp.dot(normed16, gate_weight, preferred_element_type=jnp.float32)
    gate_sig = jax.nn.sigmoid(gate_pre)
    glu = value_pre * gate_sig * mask
    conv = depthwise(glu.reshape(shards, MOST, part_width), conv_kernel).reshape(-1, part_width)
    conv_total, square_total = lax.psum(
        (jnp.sum(conv * mask, axis=0), jnp.sum(conv * conv * mask, axis=0)), "seq"
    )
    conv_mean = conv_total / count
    conv_var = square_total / count - conv_mean * conv_mean
    bn_scale = jnp.sqrt(conv_var + 1e-05)
    bn_hat = (conv - conv_mean) / bn_scale
    batch_normed = bn_gain * bn_hat + bn_shift
    bn_sig = jax.nn.sigmoid(batch_normed)
    swish = (batch_normed * bn_sig).astype(jnp.bfloat16)
    mixed = lax.psum_scatter(
        contract_cols(swish, down_weight), "tp", scatter_dimension=1, tiled=True
    )
    block_out = ((hidden_part.astype(jnp.float32) + mixed) * mask).astype(jnp.bfloat16)
    grad_out = jnp.where(valid, out_grad, jnp.zeros((), jnp.bfloat16))
    grad_full = lax.all_gather(grad_out, "tp", axis=1, tiled=True)
    down_local = contract_rows(grad_full, swish)
    grad_swish = jnp.dot(grad_full, down_weight, preferred_element_type=jnp.float32)
    grad_bn = grad_swish * bn_sig * (1.0 + batch_normed * (1.0 - bn_sig)) * mask
    bn_shift_grad, bn_gain_grad = lax.psum(
        (jnp.sum(grad_bn, axis=0), jnp.sum(grad_bn * bn_hat, axis=0)), "seq"
    )
    grad_conv = (
        bn_gain / bn_scale * (grad_bn - (bn_shift_grad + bn_hat * bn_gain_grad) / count) * mask
    )
    grad_glu = (
        depthwise_back(grad_conv.reshape(shards, MOST, part_width), conv_kernel).reshape(
            -1, part_width
        )
        * mask
    )
    grad_value = (grad_glu * gate_sig).astype(jnp.bfloat16)
    grad_gate = (grad_glu * value_pre * gate_sig * (1.0 - gate_sig)).astype(jnp.bfloat16)
    value_local = contract_rows(normed16, grad_value)
    gate_local = contract_rows(normed16, grad_gate)
    normed_terms = contract_cols(grad_value, value_weight) + contract_cols(grad_gate, gate_weight)
    grad_normed = lax.psum(normed_terms, "tp")
    grad_hidden = (
        grad_normed
        - jnp.mean(grad_normed, axis=1, keepdims=True)
        - normed * jnp.mean(grad_normed * normed, axis=1, keepdims=True)
    ) / sigma
    grad_hidden = lax.dynamic_slice_in_dim(grad_hidden, tp_index * part_width, part_width, 1)
    grad_packed = ((grad_out.astype(jnp.float32) + grad_hidden) * mask).astype(jnp.bfloat16)
    returned = lax.all_to_all(
        grad_packed.reshape(shards, MOST, part_width),
        "seq",
        split_axis=0,
        concat_axis=0,
        tiled=True,
    )
    row_ids = jnp.arange(own_rows, dtype=jnp.int32)
    clip_ends = jnp.cumsum(clip_lens)
    clip_of_row = jnp.sum((clip_ends[None, :] <= row_ids[:, None]).astype(jnp.int32), axis=1)
    row_match = clip_of_row[:, None] == shard_ids[None, :]
    row_start = jnp.sum(jnp.where(row_match, offsets[None, :], 0), axis=1)
    row_target = jnp.sum(jnp.where(row_match, clip_targets[None, :], 0), axis=1)
    positions = row_target * MOST + row_ids - row_start
    grad_proj = jnp.take(returned.reshape(shards * MOST, part_width), positions, axis=0)
    proj_local = contract_rows(subsampled, grad_proj)
    proj_grad, value_grad, gate_grad, down_grad = (
        lax.psum_scatter(proj_local, "seq", scatter_dimension=0, tiled=True),
        lax.psum_scatter(value_local, "seq", scatter_dimension=0, tiled=True),
        lax.psum_scatter(gate_local, "seq", scatter_dimension=0, tiled=True),
        lax.psum_scatter(down_local, "seq", scatter_dimension=0, tiled=True),
    )
    return (block_out, proj_grad, value_grad, gate_grad, down_grad, bn_gain_grad, bn_shift_grad)


def solution(mesh):
    placed = (
        P("seq", None),
        P(None, "tp"),
        P(None, "tp"),
        P(None, "tp"),
        P(None, "tp"),
        P("tp"),
        P("tp"),
        P(None, "tp"),
        P(),
        P(),
        P("seq", "tp"),
    )
    return jax.shard_map(
        body,
        mesh=mesh,
        in_specs=placed,
        out_specs=(
            P("seq", "tp"),
            P("seq", "tp"),
            P("seq", "tp"),
            P("seq", "tp"),
            P("seq", "tp"),
            P("tp"),
            P("tp"),
        ),
        check_vma=False,
    )
```

profile of v0, /device:TPU:0, one launch (start us, length us, event | category | flops | bytes accessed | tf_op | source)
XLA Modules:
  0.0 502.0 jit_solution(10994392400143319582)
XLA Ops:
  7.2 0.8 fusion.52
  8.1 0.2 reduce-window.4
  8.2 0.7 fusion.50
  9.0 0.1 select_reduce_fusion.4
  9.5 2.3 convolution_convert_fusion
  11.8 2.0 gather_fusion
  13.8 0.2 select_select_fusion
  14.0 16.1 %all_to_all.10 = bf16[8,64,256]{2,1,0:T(8,128)(2,1)} all-to-all(bf16[8,64,256]{2,1,0:T(8,128)(2,1)S(1)} %select_select_fusion), channel_id=1, replica_groups=mesh['seq'=8,'tp'=4] {'seq'}, dimensions={0} | all-to-all | bytes 524288 | tf_op jit(solution)/shard_map/all_to_all | solution.py:77
  30.2 0.1 select_reduce_fusion.2
  30.4 0.1 lt.106
  30.5 0.8 broadcast_select_fusion
  31.4 14.7 %all-gather.3.cloned.1.call-done = bf16[512,1024]{1,0:T(8,128)(2,1)} async-done(((bf16[512,256]{1,0:T(8,128)(2,1)}), bf16[512,1024]{1,0:T(8,128)(2,1)}) %all-gather.3.cloned.1.call-update) | async-done | bytes 1048592 | tf_op jit(solution)/shard_map/all_gather | solution.py:81
  46.1 1.5 convert_reduce_fusion
  47.6 1.6 fusion.2
  49.3 1.7 fusion.61
  51.0 0.5 fusion.6
  51.5 0.8 copy-done.6
  52.2 1.2 multiply_multiply_fusion.1
  53.5 1.5 multiply_reduce_fusion.3
  55.0 21.3 %all-reduce.3 = (f32[256]{0:T(256)S(1)}, f32[256]{0:T(256)S(1)}) all-reduce(f32[256]{0:T(256)S(1)} %get-tuple-element.31, f32[256]{0:T(256)S(1)} %get-tuple-element.30), channel_id=1, replica_groups=mesh['seq'=8,'tp'=4] {'seq'}, use_global_device_ids=true, to_apply=%region_9.10 | all-reduce | flops 512 | bytes 4096 | tf_op jit(solution)/shard_map/psum | solution.py:96
  76.3 1.9 fusion.44
  78.2 2.8 fusion.58
  81.0 17.1 %all-reduce.2 = (f32[256]{0:T(256)S(1)}, f32[256]{0:T(256)S(1)}) all-reduce(f32[256]{0:T(256)S(1)} %get-tuple-element.33, f32[256]{0:T(256)S(1)} %get-tuple-element.32), channel_id=1, replica_groups=mesh['seq'=8,'tp'=4] {'seq'}, use_global_device_ids=true, to_apply=%region_17.18 | all-reduce | flops 512 | bytes 4096 | tf_op jit(solution)/shard_map/psum | solution.py:115
  98.2 1.5 multiply_multiply_fusion
  99.7 0.5 fusion.32
  100.3 0.2 multiply_convert_fusion
  100.5 0.7 copy-done.5
  101.2 0.5 fusion.64
  101.7 1.8 convolution_add_fusion
  103.6 3.0 fusion.56
  106.7 0.1 select_reduce_fusion.1
  106.8 46.0 %all-reduce.6.cloned.1.call-done = f32[512,1024]{1,0:T(8,128)} async-done(((f32[512,1024]{1,0:T(8,128)}), f32[512,1024]{1,0:T(8,128)}) %all-reduce.6.cloned.1.call-update) | async-done | bytes 2097168 | tf_op jit(solution)/shard_map/psum | solution.py:132
  152.8 2.6 fusion.57
  155.5 31.4 %reduce-scatter.6.cloned.1.call-done = f32[512,256]{1,0:T(8,128)} async-done(((f32[512,1024]{1,0:T(8,128)}), f32[512,256]{1,0:T(8,128)}) %reduce-scatter.6.cloned.1.call-update) | async-done | bytes 524304 | tf_op jit(solution)/shard_map/reduce_scatter | solution.py:106
  186.9 2.6 fusion.45
  189.5 5.5 %all-to-all-start.1 = ((bf16[8,64,256]{2,1,0:T(8,128)(2,1)}), bf16[8,64,256]{2,1,0:T(8,128)(2,1)S(1)}, u32[]{:S(2)}, u32[]{:S(2)}) async-start(bf16[8,64,256]{2,1,0:T(8,128)(2,1)} %bitcast.70), calls=%async_computation.2 | async-start | bytes 524288 | tf_op jit(solution)/shard_map/all_to_all | solution.py:140
  195.1 8.8 %all-to-all-done.1 = bf16[8,64,256]{2,1,0:T(8,128)(2,1)S(1)} async-done(((bf16[8,64,256]{2,1,0:T(8,128)(2,1)}), bf16[8,64,256]{2,1,0:T(8,128)(2,1)S(1)}, u32[]{:S(2)}, u32[]{:S(2)}) %all-to-all-start.1) | async-done | bytes 262176 | tf_op jit(solution)/shard_map/all_to_all | solution.py:140
  203.9 1.2 gather_fusion.1
  205.1 2.7 convolution_bitcast_fusion
  207.9 0.6 copy-done.21
  208.5 2.9 fusion.55
  211.5 2.4 fusion.65
  214.0 1.5 fusion.66
  215.5 79.0 %reduce-scatter.8.cloned.1.call-done = f32[512,256]{0,1:T(8,128)} async-done(((f32[4096,256]{0,1:T(8,128)}), f32[512,256]{0,1:T(8,128)}) %reduce-scatter.8.cloned.1.call-update) | async-done | bytes 524304 | tf_op jit(solution)/shard_map/reduce_scatter | solution.py:157
  294.6 2.0 copy.20
  296.6 65.3 %reduce-scatter.14.cloned.1.call-done = f32[128,256]{1,0:T(8,128)} async-done(((f32[1024,256]{1,0:T(8,128)}), f32[128,256]{1,0:T(8,128)}) %reduce-scatter.14.cloned.1.call-update) | async-done | bytes 131088 | tf_op jit(solution)/shard_map/reduce_scatter | solution.py:160
  361.9 66.5 %reduce-scatter.10.cloned.1.call-done = f32[128,256]{1,0:T(8,128)} async-done(((f32[1024,256]{1,0:T(8,128)}), f32[128,256]{1,0:T(8,128)}) %reduce-scatter.10.cloned.1.call-update) | async-done | bytes 131088 | tf_op jit(solution)/shard_map/reduce_scatter | solution.py:158
  428.4 66.8 %reduce-scatter.12.cloned.1.call-done = f32[128,256]{1,0:T(8,128)} async-done(((f32[1024,256]{1,0:T(8,128)}), f32[128,256]{1,0:T(8,128)}) %reduce-scatter.12.cloned.1.call-update) | async-done | bytes 131088 | tf_op jit(solution)/shard_map/reduce_scatter | solution.py:159
  (77 shorter events, 1.1 us)
Async XLA Ops:
  7.2 2.3 copy-start
  7.2 38.9 %all-gather.3.cloned.1.call-start = ((), (), s32[]{:S(2)}) async-start(), calls=%async_computation.7 | async-start | bytes 1310720 | tf_op jit(solution)/shard_map/all_gather | solution.py:81
  11.8 18.4 %copy-start.15 = (s32[8,8]{1,0:T(8,128)S(1)}, s32[8,8]{1,0:T(8,128)}, u32[]{:S(2)}) copy-start(s32[8,8]{1,0:T(8,128)} %param.19) | copy-start | bytes 772
  11.8 18.4 %copy-start.16 = (s32[8,8]{1,0:T(8,128)S(1)}, s32[8,8]{1,0:T(8,128)}, u32[]{:S(2)}) copy-start(s32[8,8]{1,0:T(8,128)} %param.20) | copy-start | bytes 772
  11.8 18.7 %copy-start.11 = (bf16[512,256]{1,0:T(8,128)(2,1)S(1)}, bf16[512,256]{1,0:T(8,128)(2,1)}, u32[]{:S(2)}) copy-start(bf16[512,256]{1,0:T(8,128)(2,1)} %param.21) | copy-start | bytes 786436
  11.8 19.6 %copy-start.14 = (f32[9,256]{1,0:T(8,128)S(1)}, f32[9,256]{1,0:T(8,128)}, u32[]{:S(2)}) copy-start(f32[9,256]{1,0:T(8,128)} %param.15) | copy-start | bytes 27652
  30.1 48.1 %all-gather.5.cloned.1.call-start = ((), (), s32[]{:S(2)}) async-start(), calls=%async_computation.9 | async-start | bytes 1310720 | tf_op jit(solution)/shard_map/all_gather | solution.py:111
  31.3 121.5 %all-reduce.6.cloned.1.call-start = ((), (), s32[]{:S(2)}) async-start(), calls=%async_computation.10 | async-start | bytes 4194304 | tf_op jit(solution)/shard_map/psum | solution.py:132
  46.1 3.2 copy-start.1
  49.3 1.7 copy-start.12
  51.0 1.3 copy-start.9
  51.4 0.8 copy-start.6
  52.2 24.1 %copy-start.17 = (f32[256]{0:T(256)S(1)}, f32[256]{0:T(256)}, u32[]{:S(2)}) copy-start(f32[256]{0:T(256)} %param.16) | copy-start | bytes 3076
  52.2 26.0 %copy-start.20 = (f32[256]{0:T(256)S(1)}, f32[256]{0:T(256)}, u32[]{:S(2)}) copy-start(f32[256]{0:T(256)} %param.17) | copy-start | bytes 3076
  98.2 2.3 copy-start.18
  98.2 2.3 copy-start.19
  98.2 2.1 copy-start.7
  98.2 2.1 copy-start.8
  98.2 3.0 copy-start.10
  100.2 1.4 copy-start.13
  100.5 0.7 copy-start.5
  100.5 1.2 copy-start.2
  103.5 83.4 %reduce-scatter.6.cloned.1.call-start = ((), (), s32[]{:S(2)}) async-start(), calls=%async_computation.8 | async-start | bytes 2621440 | tf_op jit(solution)/shard_map/reduce_scatter | solution.py:106
  152.8 34.1 %copy-start.4 = (bf16[8,64,256]{2,1,0:T(8,128)(2,1)S(1)}, bf16[8,64,256]{2,1,0:T(8,128)(2,1)}, u32[]{:S(2)}) copy-start(bf16[8,64,256]{2,1,0:T(8,128)(2,1)} %all_to_all.10) | copy-start | bytes 786436
  189.5 14.4 %all-to-all-start.1 = ((bf16[8,64,256]{2,1,0:T(8,128)(2,1)}), bf16[8,64,256]{2,1,0:T(8,128)(2,1)S(1)}, u32[]{:S(2)}, u32[]{:S(2)}) async-start(bf16[8,64,256]{2,1,0:T(8,128)(2,1)} %bitcast.70), calls=%async_computation.2 | async-start | bytes 524288 | tf_op jit(solution)/shard_map/all_to_all | solution.py:140
  195.0 99.5 %reduce-scatter.8.cloned.1.call-start = ((), (), s32[]{:S(2)}) async-start(), calls=%async_computation.11 | async-start | bytes 4718592 | tf_op jit(solution)/shard_map/reduce_scatter | solution.py:157
  207.8 0.7 copy-start.21
  207.9 154.0 %reduce-scatter.14.cloned.1.call-start = ((), (), s32[]{:S(2)}) async-start(), calls=%async_computation.14 | async-start | bytes 1179648 | tf_op jit(solution)/shard_map/reduce_scatter | solution.py:160
  211.4 2.6 copy-start.3
  211.5 216.9 %reduce-scatter.10.cloned.1.call-start = ((), (), s32[]{:S(2)}) async-start(), calls=%async_computation.12 | async-start | bytes 1179648 | tf_op jit(solution)/shard_map/reduce_scatter | solution.py:158
  214.0 281.2 %reduce-scatter.12.cloned.1.call-start = ((), (), s32[]{:S(2)}) async-start(), calls=%async_computation.13 | async-start | bytes 1179648 | tf_op jit(solution)/shard_map/reduce_scatter | solution.py:159
Sparse Core Ops, SparseCore 0:
  30.2 15.8 all-gather.2
  48.2 16.8 all-gather.4
  103.6 49.1 all-reduce.5
  155.4 31.4 reduce-scatter.5
  208.0 86.5 reduce-scatter.7
  298.8 63.0 reduce-scatter.13
  365.9 62.4 reduce-scatter.9
  432.7 62.3 reduce-scatter.11
where the time goes:
time: 503 us; the launch traced here: 502 us
  waiting for transfers between devices  379 us (75%)
  blocking collectives  54.6 us (11%)
  matrix products  21.7 us (4%)
  other arithmetic  18.4 us (4%)
  between operations  14.5 us (3%)
  local copies, waits for them, and re-layouts  8.33 us (2%)
  starting transfers between devices  5.84 us (1%)
    reduce_scatter x1, waiting for transfers between devices, body(): lax.psum_scatter(proj_local, 'seq', scatter_dimension=0, tiled=True)  79 us
    reduce_scatter x1, waiting for transfers between devices, body(): lax.psum_scatter(gate_local, 'seq', scatter_dimension=0, tiled=True)  66.8 us
    reduce_scatter x1, waiting for transfers between devices, body(): lax.psum_scatter(value_local, 'seq', scatter_dimension=0, tiled=True)  66.5 us
    reduce_scatter x1, waiting for transfers between devices, body(): lax.psum_scatter(down_local, 'seq', scatter_dimension=0, tiled=True)  65.3 us
    psum x1, waiting for transfers between devices, body(): grad_normed = lax.psum(normed_terms, 'tp')  46 us
    reduce_scatter x1, waiting for transfers between devices, body(): lax.psum_scatter(contract_cols(swish, down_weight), 'tp', scatter_dimensi...  31.4 us
    psum x1, blocking collectives, body(): lax.psum((jnp.sum(conv * mask, axis=0), jnp.sum(conv * conv * mask, axis=...  21.3 us
    psum x1, blocking collectives, body(): lax.psum((jnp.sum(grad_bn, axis=0), jnp.sum(grad_bn * bn_hat, axis=0)), '...  17.1 us
  transfers between devices with their start and end apart: 9, of which 8 were waited for; matrix products, arithmetic and copies ran while one was open for 5% of the time, Pallas kernels for 0%

commit v1 on v0

--- a/solution.py
+++ b/solution.py
@@ -4,6 +4,18 @@
 from jax.sharding import PartitionSpec as P
 
 MOST = 64
+
+
+def rotated_exchange(x, axis, split, join):
+    ways, here = (lax.axis_size(axis), lax.axis_index(axis))
+    width = x.shape[split] // ways
+    turned = jnp.roll(x, -here * width, axis=split)
+    got = [lax.slice_in_dim(turned, 0, width, axis=split)]
+    for far in range(1, ways):
+        sent = lax.slice_in_dim(turned, far * width, (far + 1) * width, axis=split)
+        got.append(lax.ppermute(sent, axis, [(d, (d + far) % ways) for d in range(ways)]))
+    line = jnp.concatenate(got[::-1], axis=join)
+    return jnp.roll(line, (here + 1) * got[0].shape[join], axis=join)
 
 
 def depthwise(field, kernel):
@@ -74,9 +86,7 @@
     outgoing = jnp.where(
         send_valid, jnp.take(projected, source_rows, axis=0), jnp.zeros((), jnp.bfloat16)
     )
-    arrived = lax.all_to_all(
-        outgoing.reshape(shards, MOST, part_width), "seq", split_axis=0, concat_axis=0, tiled=True
-    )
+    arrived = rotated_exchange(outgoing.reshape(shards, MOST, part_width), "seq", 0, 0)
     hidden_part = arrived.reshape(shards * MOST, part_width)
     hidden_full = lax.all_gather(hidden_part, "tp", axis=1, tiled=True)
     incoming = clip_dest == seq_index

time: 503 us -> 512 us (1.018)
  blocking collectives: 54.6 us -> 38.5 us
  starting transfers between devices: 5.84 us -> 20.7 us
  waiting for transfers between devices: 379 us -> 388 us
    all_to_all x1 -> x0, blocking collectives: 16.1 us -> none  [body(): lax.all_to_all(outgoing.reshape(shards, MOST, part_width), 'seq', split_a...]
    ppermute x0 -> x7, starting transfers between devices: none -> 14.9 us  [rotated_exchange(): lax.ppermute(sent, axis, [(d, (d + far) % ways) for d in range(ways)])]
    ppermute x0 -> x7, waiting for transfers between devices: none -> 5.78 us  [rotated_exchange(): lax.ppermute(sent, axis, [(d, (d + far) % ways) for d in range(ways)])]
  transfers between devices with their start and end apart: 9 -> 16, of which waited for: 8 -> 10; matrix products, arithmetic and copies ran while one was open for 5% -> 5% of each run, Pallas kernels for 0% -> 0%
where the time goes in v1:
time: 512 us; the launch traced here: 511 us
  waiting for transfers between devices  388 us (76%)
  blocking collectives  38.5 us (8%)
  matrix products  21.7 us (4%)
  starting transfers between devices  20.7 us (4%)
  other arithmetic  19.3 us (4%)
  between operations  14.6 us (3%)
  local copies, waits for them, and re-layouts  8.39 us (2%)
    reduce_scatter x1, waiting for transfers between devices, body(): lax.psum_scatter(proj_local, 'seq', scatter_dimension=0, tiled=True)  79 us
    reduce_scatter x1, waiting for transfers between devices, body(): lax.psum_scatter(gate_local, 'seq', scatter_dimension=0, tiled=True)  66.9 us
    reduce_scatter x1, waiting for transfers between devices, body(): lax.psum_scatter(value_local, 'seq', scatter_dimension=0, tiled=True)  66.5 us
    reduce_scatter x1, waiting for transfers between devices, body(): lax.psum_scatter(down_local, 'seq', scatter_dimension=0, tiled=True)  65.4 us
    psum x1, waiting for transfers between devices, body(): grad_normed = lax.psum(normed_terms, 'tp')  46 us
    reduce_scatter x1, waiting for transfers between devices, body(): lax.psum_scatter(contract_cols(swish, down_weight), 'tp', scatter_dimensi...  31.4 us
    psum x1, blocking collectives, body(): lax.psum((jnp.sum(conv * mask, axis=0), jnp.sum(conv * conv * mask, axis=...  21.3 us
    all_gather x1, waiting for transfers between devices, body(): hidden_full = lax.all_gather(hidden_part, 'tp', axis=1, tiled=True)  18.3 us
  transfers between devices with their start and end apart: 16, of which 10 were waited for; matrix products, arithmetic and copies ran while one was open for 5% of the time, Pallas kernels for 0%

profile of v1, /device:TPU:0, one launch (start us, length us, event | category | flops | bytes accessed | tf_op | source)
XLA Modules:
  0.0 511.5 jit_solution(2045455336694640252)
XLA Ops:
  7.2 0.8 fusion.54
  8.3 0.7 fusion.52
  9.5 2.3 convolution_convert_fusion
  11.8 2.0 gather_fusion
  14.2 6.1 %collective-permute-start = (bf16[1,64,256]{2,1,0:T(8,128)(2,1)S(1)}, bf16[1,64,256]{2,1,0:T(8,128)(2,1)S(1)}, u32[]{:S(2)}, u32[]{:S(2)}) collective-permute-start(bf16[1,64,256]{2,1,0:T(8,128)(2,1)S(1)} %get-tuple-element.56), channel_id=1, source_target_pairs={{0,28},{4,0},{8,4},{12,8},{16,12},{20,16},{24,20},{28,24},{1,29},{... | collective-permute-start | bytes 98312 | tf_op jit(solution)/shard_map/ppermute | solution.py:16
  20.2 2.5 collective-permute-start.4
  22.7 2.8 collective-permute-start.3
  25.5 2.9 collective-permute-start.1
  28.4 1.6 collective-permute-done.1
  30.0 0.6 collective-permute-start.2
  30.7 4.2 collective-permute-done.2
  34.9 0.8 fusion.46
  36.1 0.8 broadcast_select_fusion
  37.1 18.3 %all-gather.3.cloned.1.call-done = bf16[512,1024]{1,0:T(8,128)(2,1)} async-done(((bf16[512,256]{1,0:T(8,128)(2,1)}), bf16[512,1024]{1,0:T(8,128)(2,1)}) %all-gather.3.cloned.1.call-update) | async-done | bytes 1048592 | tf_op jit(solution)/shard_map/all_gather | solution.py:91
  55.4 1.5 convert_reduce_fusion
  56.9 1.6 fusion.2
  58.6 1.7 fusion.63
  60.2 0.5 fusion.6
  60.7 0.8 copy-done.6
  61.5 1.2 multiply_multiply_fusion.1
  62.7 1.5 multiply_reduce_fusion.3
  64.2 21.3 %all-reduce.3 = (f32[256]{0:T(256)S(1)}, f32[256]{0:T(256)S(1)}) all-reduce(f32[256]{0:T(256)S(1)} %get-tuple-element.32, f32[256]{0:T(256)S(1)} %get-tuple-element.31), channel_id=1, replica_groups=mesh['seq'=8,'tp'=4] {'seq'}, use_global_device_ids=true, to_apply=%region_9.11 | all-reduce | flops 512 | bytes 4096 | tf_op jit(solution)/shard_map/psum | solution.py:106
  85.5 1.9 fusion.44
  87.4 2.8 fusion.60
  90.3 17.1 %all-reduce.2 = (f32[256]{0:T(256)S(1)}, f32[256]{0:T(256)S(1)}) all-reduce(f32[256]{0:T(256)S(1)} %get-tuple-element.34, f32[256]{0:T(256)S(1)} %get-tuple-element.33), channel_id=1, replica_groups=mesh['seq'=8,'tp'=4] {'seq'}, use_global_device_ids=true, to_apply=%region_17.19 | all-reduce | flops 512 | bytes 4096 | tf_op jit(solution)/shard_map/psum | solution.py:125
  107.4 1.5 multiply_multiply_fusion
  108.9 0.5 fusion.32
  109.7 0.7 copy-done.5
  110.4 0.5 fusion.67
  110.9 1.8 convolution_add_fusion
  112.8 3.0 fusion.58
  116.0 46.0 %all-reduce.6.cloned.1.call-done = f32[512,1024]{1,0:T(8,128)} async-done(((f32[512,1024]{1,0:T(8,128)}), f32[512,1024]{1,0:T(8,128)}) %all-reduce.6.cloned.1.call-update) | async-done | bytes 2097168 | tf_op jit(solution)/shard_map/psum | solution.py:142
  162.1 2.6 fusion.59
  164.7 31.4 %reduce-scatter.6.cloned.1.call-done = f32[512,256]{1,0:T(8,128)} async-done(((f32[512,1024]{1,0:T(8,128)}), f32[512,256]{1,0:T(8,128)}) %reduce-scatter.6.cloned.1.call-update) | async-done | bytes 524304 | tf_op jit(solution)/shard_map/reduce_scatter | solution.py:116
  196.1 2.6 fusion.45
  198.8 5.5 %all-to-all-start = ((bf16[8,64,256]{2,1,0:T(8,128)(2,1)}), bf16[8,64,256]{2,1,0:T(8,128)(2,1)S(1)}, u32[]{:S(2)}, u32[]{:S(2)}) async-start(bf16[8,64,256]{2,1,0:T(8,128)(2,1)} %bitcast.70), calls=%async_computation.1 | async-start | bytes 524288 | tf_op jit(solution)/shard_map/all_to_all | solution.py:150
  204.4 8.8 %all-to-all-done = bf16[8,64,256]{2,1,0:T(8,128)(2,1)S(1)} async-done(((bf16[8,64,256]{2,1,0:T(8,128)(2,1)}), bf16[8,64,256]{2,1,0:T(8,128)(2,1)S(1)}, u32[]{:S(2)}, u32[]{:S(2)}) %all-to-all-start) | async-done | bytes 262176 | tf_op jit(solution)/shard_map/all_to_all | solution.py:150
  213.2 1.2 gather_fusion.1
  214.3 2.8 convolution_bitcast_fusion
  217.2 0.6 copy-done.21
  217.8 2.9 fusion.57
  220.8 2.4 fusion.68
  223.3 1.5 fusion.69
  224.8 79.0 %reduce-scatter.8.cloned.1.call-done = f32[512,256]{0,1:T(8,128)} async-done(((f32[4096,256]{0,1:T(8,128)}), f32[512,256]{0,1:T(8,128)}) %reduce-scatter.8.cloned.1.call-update) | async-done | bytes 524304 | tf_op jit(solution)/shard_map/reduce_scatter | solution.py:167
  303.8 2.0 copy.20
  305.8 65.4 %reduce-scatter.14.cloned.1.call-done = f32[128,256]{1,0:T(8,128)} async-done(((f32[1024,256]{1,0:T(8,128)}), f32[128,256]{1,0:T(8,128)}) %reduce-scatter.14.cloned.1.call-update) | async-done | bytes 131088 | tf_op jit(solution)/shard_map/reduce_scatter | solution.py:170
  371.2 66.5 %reduce-scatter.10.cloned.1.call-done = f32[128,256]{1,0:T(8,128)} async-done(((f32[1024,256]{1,0:T(8,128)}), f32[128,256]{1,0:T(8,128)}) %reduce-scatter.10.cloned.1.call-update) | async-done | bytes 131088 | tf_op jit(solution)/shard_map/reduce_scatter | solution.py:168
  437.7 66.9 %reduce-scatter.12.cloned.1.call-done = f32[128,256]{1,0:T(8,128)} async-done(((f32[1024,256]{1,0:T(8,128)}), f32[128,256]{1,0:T(8,128)}) %reduce-scatter.12.cloned.1.call-update) | async-done | bytes 131088 | tf_op jit(solution)/shard_map/reduce_scatter | solution.py:169
  (101 shorter events, 2.3 us)
Async XLA Ops:
  7.2 2.3 copy-start
  7.2 48.2 %all-gather.3.cloned.1.call-start = ((), (), s32[]{:S(2)}) async-start(), calls=%async_computation.6 | async-start | bytes 1310720 | tf_op jit(solution)/shard_map/all_gather | solution.py:91
  11.8 24.0 %copy-start.15 = (s32[8,8]{1,0:T(8,128)S(1)}, s32[8,8]{1,0:T(8,128)}, u32[]{:S(2)}) copy-start(s32[8,8]{1,0:T(8,128)} %param.21) | copy-start | bytes 772
  11.8 24.0 %copy-start.16 = (s32[8,8]{1,0:T(8,128)S(1)}, s32[8,8]{1,0:T(8,128)}, u32[]{:S(2)}) copy-start(s32[8,8]{1,0:T(8,128)} %param.22) | copy-start | bytes 772
  11.8 24.3 %copy-start.11 = (bf16[512,256]{1,0:T(8,128)(2,1)S(1)}, bf16[512,256]{1,0:T(8,128)(2,1)}, u32[]{:S(2)}) copy-start(bf16[512,256]{1,0:T(8,128)(2,1)} %param.23) | copy-start | bytes 786436
  13.8 23.3 %copy-start.14 = (f32[9,256]{1,0:T(8,128)S(1)}, f32[9,256]{1,0:T(8,128)}, u32[]{:S(2)}) copy-start(f32[9,256]{1,0:T(8,128)} %param.17) | copy-start | bytes 27652
  14.2 11.4 %collective-permute-start = (bf16[1,64,256]{2,1,0:T(8,128)(2,1)S(1)}, bf16[1,64,256]{2,1,0:T(8,128)(2,1)S(1)}, u32[]{:S(2)}, u32[]{:S(2)}) collective-permute-start(bf16[1,64,256]{2,1,0:T(8,128)(2,1)S(1)} %get-tuple-element.56), channel_id=1, source_target_pairs={{0,28},{4,0},{8,4},{12,8},{16,12},{20,16},{24,20},{28,24},{1,29},{... | collective-permute-start | bytes 98312 | tf_op jit(solution)/shard_map/ppermute | solution.py:16
  20.2 14.7 %collective-permute-start.6 = (bf16[1,64,256]{2,1,0:T(8,128)(2,1)S(1)}, bf16[1,64,256]{2,1,0:T(8,128)(2,1)S(1)}, u32[]{:S(2)}, u32[]{:S(2)}) collective-permute-start(bf16[1,64,256]{2,1,0:T(8,128)(2,1)S(1)} %get-tuple-element.50), channel_id=1, source_target_pairs={{0,4},{4,8},{8,12},{12,16},{16,20},{20,24},{24,28},{28,0},{1,5},{5... | collective-permute-start | bytes 98312 | tf_op jit(solution)/shard_map/ppermute | solution.py:16
  20.2 14.7 %collective-permute-start.5 = (bf16[1,64,256]{2,1,0:T(8,128)(2,1)S(1)}, bf16[1,64,256]{2,1,0:T(8,128)(2,1)S(1)}, u32[]{:S(2)}, u32[]{:S(2)}) collective-permute-start(bf16[1,64,256]{2,1,0:T(8,128)(2,1)S(1)} %get-tuple-element.51), channel_id=1, source_target_pairs={{0,8},{4,12},{8,16},{12,20},{16,24},{20,28},{24,0},{28,4},{1,9},{5... | collective-permute-start | bytes 98312 | tf_op jit(solution)/shard_map/ppermute | solution.py:16
  20.2 14.6 %collective-permute-start.4 = (bf16[1,64,256]{2,1,0:T(8,128)(2,1)S(1)}, bf16[1,64,256]{2,1,0:T(8,128)(2,1)S(1)}, u32[]{:S(2)}, u32[]{:S(2)}) collective-permute-start(bf16[1,64,256]{2,1,0:T(8,128)(2,1)S(1)} %get-tuple-element.52), channel_id=1, source_target_pairs={{0,12},{4,16},{8,20},{12,24},{16,28},{20,0},{24,4},{28,8},{1,13},{... | collective-permute-start | bytes 98312 | tf_op jit(solution)/shard_map/ppermute | solution.py:16
  22.7 12.2 %collective-permute-start.3 = (bf16[1,64,256]{2,1,0:T(8,128)(2,1)S(1)}, bf16[1,64,256]{2,1,0:T(8,128)(2,1)S(1)}, u32[]{:S(2)}, u32[]{:S(2)}) collective-permute-start(bf16[1,64,256]{2,1,0:T(8,128)(2,1)S(1)} %get-tuple-element.53), channel_id=1, source_target_pairs={{0,16},{4,20},{8,24},{12,28},{16,0},{20,4},{24,8},{28,12},{1,17},{... | collective-permute-start | bytes 98312 | tf_op jit(solution)/shard_map/ppermute | solution.py:16
  25.5 4.5 collective-permute-start.1
  30.0 4.8 collective-permute-start.2
  35.8 51.7 %all-gather.5.cloned.1.call-start = ((), (), s32[]{:S(2)}) async-start(), calls=%async_computation.8 | async-start | bytes 1310720 | tf_op jit(solution)/shard_map/all_gather | solution.py:121
  37.0 125.1 %all-reduce.6.cloned.1.call-start = ((), (), s32[]{:S(2)}) async-start(), calls=%async_computation.9 | async-start | bytes 4194304 | tf_op jit(solution)/shard_map/psum | solution.py:142
  55.4 3.2 copy-start.1
  58.6 1.7 copy-start.12
  60.2 1.3 copy-start.9
  60.7 0.8 copy-start.6
  61.5 24.0 %copy-start.17 = (f32[256]{0:T(256)S(1)}, f32[256]{0:T(256)}, u32[]{:S(2)}) copy-start(f32[256]{0:T(256)} %param.18) | copy-start | bytes 3076
  61.5 25.9 %copy-start.20 = (f32[256]{0:T(256)S(1)}, f32[256]{0:T(256)}, u32[]{:S(2)}) copy-start(f32[256]{0:T(256)} %param.19) | copy-start | bytes 3076
  107.4 2.3 copy-start.18
  107.4 2.3 copy-start.19
  107.4 2.1 copy-start.7
  107.4 2.1 copy-start.8
  107.4 3.0 copy-start.10
  109.5 1.4 copy-start.13
  109.7 0.7 copy-start.5
  109.7 1.2 copy-start.2
  112.8 83.4 %reduce-scatter.6.cloned.1.call-start = ((), (), s32[]{:S(2)}) async-start(), calls=%async_computation.7 | async-start | bytes 2621440 | tf_op jit(solution)/shard_map/reduce_scatter | solution.py:116
  162.1 34.1 %copy-start.4 = (bf16[8,64,256]{2,1,0:T(8,128)(2,1)S(1)}, bf16[8,64,256]{2,1,0:T(8,128)(2,1)}, u32[]{:S(2)}) copy-start(bf16[8,64,256]{2,1,0:T(8,128)(2,1)} %fusion.46) | copy-start | bytes 786436
  198.8 14.4 %all-to-all-start = ((bf16[8,64,256]{2,1,0:T(8,128)(2,1)}), bf16[8,64,256]{2,1,0:T(8,128)(2,1)S(1)}, u32[]{:S(2)}, u32[]{:S(2)}) async-start(bf16[8,64,256]{2,1,0:T(8,128)(2,1)} %bitcast.70), calls=%async_computation.1 | async-start | bytes 524288 | tf_op jit(solution)/shard_map/all_to_all | solution.py:150
  204.3 99.5 %reduce-scatter.8.cloned.1.call-start = ((), (), s32[]{:S(2)}) async-start(), calls=%async_computation.10 | async-start | bytes 4718592 | tf_op jit(solution)/shard_map/reduce_scatter | solution.py:167
  217.1 0.7 copy-start.21
  217.1 154.1 %reduce-scatter.14.cloned.1.call-start = ((), (), s32[]{:S(2)}) async-start(), calls=%async_computation.13 | async-start | bytes 1179648 | tf_op jit(solution)/shard_map/reduce_scatter | solution.py:170
  220.7 2.6 copy-start.3
  220.7 217.0 %reduce-scatter.10.cloned.1.call-start = ((), (), s32[]{:S(2)}) async-start(), calls=%async_computation.11 | async-start | bytes 1179648 | tf_op jit(solution)/shard_map/reduce_scatter | solution.py:168
  223.2 281.4 %reduce-scatter.12.cloned.1.call-start = ((), (), s32[]{:S(2)}) async-start(), calls=%async_computation.12 | async-start | bytes 1179648 | tf_op jit(solution)/shard_map/reduce_scatter | solution.py:169
Sparse Core Ops, SparseCore 0:
  35.9 19.4 all-gather.2
  56.9 16.8 all-gather.4
  112.9 49.1 all-reduce.5
  164.6 31.4 reduce-scatter.5
  217.2 86.5 reduce-scatter.7
  308.0 63.1 reduce-scatter.13
  375.2 62.4 reduce-scatter.9
  442.1 62.4 reduce-scatter.11
